TPU v7x, 1024 devices: a whole 4x4x32 slice. The times are simulated.
1024 devices in a mesh: node: 8 (over x, core), local: 32 (over z), dp: 4 (over y).
Axes of the slice: x: 4, y: 4, z: 32, core: 2. Of those that a mesh axis runs over, the one named last changes fastest.
Arguments:
- grad_out: bfloat16 [24576, 3584], P(('node', 'local', 'dp')), may hold values from -6 to 6
- expert_ids: int32 [24576, 8], P(('node', 'local', 'dp')), may hold values from 0 to 255, as said below
- slot_ids: int32 [24576, 8], P(('node', 'local', 'dp')), may hold values from -1 to 5, as said below
- gate_values: bfloat16 [24576, 8], P(('node', 'local', 'dp')), may hold values from 0.049804688 to 0.59765625
- hidden: bfloat16 [256, 768, 1024], P(('node', 'local'), 'dp'), may hold values from -0.59765625 to 0.59765625
Outputs:
- grad_weight: bfloat16 [256, 3584, 1024], P(('node', 'local'), 'dp')
Inputs may be any that keep to these rules, and one draw needn't show every extreme that they name: `expert_ids`: each row names 8 different experts, which lie in at most 4 groups; expert e belongs to group e // 32. For one expert and the tokens of all devices that share a local index and a dp index, the assignments with slot_ids >= 0 have different slots; -1 marks a dropped assignment. In every dp replica some expert has all 6 slots filled for every local index.
All inputs are finite; a program needn't handle non-finite values.
Results may differ from a plain program's by a relative error of at most 0.013.
Values may be sent and summed in bfloat16 or wider, within the bound.
A program may use at most 32 MiB of HBM per device.

v0:
```python
import jax
import jax.numpy as jnp
from jax import lax
from jax.sharding import PartitionSpec as P


def shards(grad_out, expert_ids, slot_ids, gate_values, hidden):
    node_count = lax.axis_size("node")
    local_count = lax.axis_size("local")
    tok_count, features = grad_out.shape
    top_count = expert_ids.shape[1]
    capacity = hidden.shape[1]
    block_slots = capacity // local_count
    node_ids = jnp.arange(node_count, dtype=jnp.int32)
    slot_code = expert_ids % local_count * block_slots + slot_ids
    for_group = ((expert_ids // local_count)[None, :, :] == node_ids[:, None, None]) & (
        slot_ids >= 0
    )[None, :, :]
    chosen = jnp.any(for_group, axis=2)
    outgoing = jnp.where(chosen[:, :, None], grad_out[None, :, :], jnp.zeros((), jnp.bfloat16))
    codes_out = jnp.where(for_group, slot_code[None, :, :], -1)
    gates_out = jnp.where(for_group, gate_values[None, :, :], jnp.zeros((), jnp.bfloat16))
    arrived_rows, arrived_codes, arrived_gates = (
        lax.all_to_all(outgoing, "node", split_axis=0, concat_axis=0, tiled=True),
        lax.all_to_all(codes_out, "node", split_axis=0, concat_axis=0, tiled=True),
        lax.all_to_all(gates_out, "node", split_axis=0, concat_axis=0, tiled=True),
    )
    arrived_rows = arrived_rows.reshape(node_count * tok_count, features)
    arrived_codes = arrived_codes.reshape(node_count * tok_count, top_count)
    arrived_gates = arrived_gates.reshape(node_count * tok_count, top_count)
    positions = jnp.arange(capacity, dtype=jnp.int32)
    matches = arrived_codes[None, :, :] == positions[:, None, None]
    placement = jnp.any(matches, axis=2).astype(jnp.bfloat16)
    bucket = jnp.dot(placement, arrived_rows, preferred_element_type=jnp.float32).astype(
        jnp.bfloat16
    )
    bucket_gates = jnp.sum(
        jnp.where(matches, arrived_gates[None, :, :].astype(jnp.float32), 0.0), axis=(1, 2)
    ).astype(jnp.bfloat16)
    expert_rows, slot_gates = (
        lax.all_to_all(
            bucket.reshape(local_count, block_slots, features),
            "local",
            split_axis=0,
            concat_axis=0,
            tiled=True,
        ),
        lax.all_to_all(
            bucket_gates.reshape(local_count, block_slots),
            "local",
            split_axis=0,
            concat_axis=0,
            tiled=True,
        ),
    )
    expert_rows = expert_rows.reshape(capacity, features)
    slot_gates = slot_gates.reshape(capacity)
    scaled = (slot_gates.astype(jnp.float32)[:, None] * hidden[0].astype(jnp.float32)).astype(
        jnp.bfloat16
    )
    summed = lax.psum_scatter(
        lax.dot_general(
            expert_rows, scaled, (((0,), (0,)), ((), ())), preferred_element_type=jnp.float32
        ).astype(jnp.bfloat16),
        "dp",
        scatter_dimension=0,
        tiled=True,
    )
    return summed[None, :, :]


def solution(mesh):
    in_specs = (
        P(("node", "local", "dp"), None),
        P(("node", "local", "dp"), None),
        P(("node", "local", "dp"), None),
        P(("node", "local", "dp"), None),
        P(("node", "local"), "dp", None),
    )
    out_specs = P(("node", "local"), "dp", None)
    return jax.shard_map(shards, mesh=mesh, in_specs=in_specs, out_specs=out_specs, check_vma=False)
```

profile of v0, /device:TPU:1, one launch (start us, length us, event | category | flops | bytes accessed | tf_op | source)
XLA Modules:
  0.0 366.0 jit_solution(14427499056909256686)
XLA Ops:
  6.5 0.7 broadcast_compare_fusion
  7.2 0.7 add_select_fusion.1
  7.9 1.3 fusion.5
  9.2 17.4 %all-to-all-start.3 = ((bf16[8,24,8]{1,2,0:T(8,128)(2,1)}), bf16[8,24,8]{1,2,0:T(8,128)(2,1)S(1)}, u32[]{:S(2)}, u32[]{:S(2)}) async-start(bf16[8,24,8]{1,2,0:T(8,128)(2,1)} %fusion.5), calls=%async_computation.3 | async-start | bytes 32768 | tf_op jit(solution)/shard_map/all_to_all | solution.py:26
  26.7 0.7 reshape.69
  27.4 3.9 %all-to-all-done.3 = bf16[8,24,8]{1,2,0:T(8,128)(2,1)S(1)} async-done(((bf16[8,24,8]{1,2,0:T(8,128)(2,1)}), bf16[8,24,8]{1,2,0:T(8,128)(2,1)S(1)}, u32[]{:S(2)}, u32[]{:S(2)}) %all-to-all-start.3) | async-done | bytes 3104 | tf_op jit(solution)/shard_map/all_to_all | solution.py:26
  31.3 3.9 %all-to-all-start = ((s32[8,1,192]{2,1,0:T(1,128)}), s32[8,1,192]{2,1,0:T(1,128)S(1)}, u32[]{:S(2)}, u32[]{:S(2)}) async-start(s32[8,1,192]{2,1,0:T(1,128)} %reshape.69), calls=%async_computation | async-start | bytes 16384 | tf_op jit(solution)/shard_map/all_to_all | solution.py:25
  35.2 2.2 broadcast_select_fusion
  37.4 2.5 all-to-all-done
  39.9 4.2 %all-to-all-start.1 = ((bf16[8,24,3584]{2,1,0:T(8,128)(2,1)}), bf16[8,24,3584]{2,1,0:T(8,128)(2,1)S(1)}, u32[]{:S(2)}, u32[]{:S(2)}) async-start(bf16[8,24,3584]{2,1,0:T(8,128)(2,1)} %broadcast_select_fusion), calls=%async_computation.1 | async-start | bytes 2752512 | tf_op jit(solution)/shard_map/all_to_all | solution.py:24
  44.1 0.6 broadcast.27
  44.7 0.7 reduce.4
  45.6 1.0 select_reduce_fusion
  46.7 0.7 convert_element_type.65
  47.4 0.6 fusion
  47.9 14.8 %all-to-all-done.1 = bf16[8,24,3584]{2,1,0:T(8,128)(2,1)S(1)} async-done(((bf16[8,24,3584]{2,1,0:T(8,128)(2,1)}), bf16[8,24,3584]{2,1,0:T(8,128)(2,1)S(1)}, u32[]{:S(2)}, u32[]{:S(2)}) %all-to-all-start.1) | async-done | bytes 1376288 | tf_op jit(solution)/shard_map/all_to_all | solution.py:24
  62.7 16.8 %all-to-all-start.4 = ((bf16[32,1,6]{2,1,0:T(2,128)(2,1)}), bf16[32,1,6]{2,1,0:T(2,128)(2,1)S(1)}, u32[]{:S(2)}, u32[]{:S(2)}) async-start(bf16[32,1,6]{2,1,0:T(2,128)(2,1)} %convert_element_type.65), calls=%async_computation.4 | async-start | bytes 32768 | tf_op jit(solution)/shard_map/all_to_all | solution.py:48
  79.5 0.5 convolution_convert_fusion.1
  80.1 1.5 reshape.58
  81.5 19.3 %all-to-all-done.4 = bf16[32,1,6]{2,1,0:T(2,128)(2,1)S(1)} async-done(((bf16[32,1,6]{2,1,0:T(2,128)(2,1)}), bf16[32,1,6]{2,1,0:T(2,128)(2,1)S(1)}, u32[]{:S(2)}, u32[]{:S(2)}) %all-to-all-start.4) | async-done | bytes 416 | tf_op jit(solution)/shard_map/all_to_all | solution.py:48
  100.8 4.0 %all-to-all-start.2 = ((bf16[32,6,3584]{2,1,0:T(8,128)(2,1)}), bf16[32,6,3584]{2,1,0:T(8,128)(2,1)S(1)}, u32[]{:S(2)}, u32[]{:S(2)}) async-start(bf16[32,6,3584]{2,1,0:T(8,128)(2,1)} %reshape.58), calls=%async_computation.2 | async-start | bytes 3670016 | tf_op jit(solution)/shard_map/all_to_all | solution.py:41
  105.0 169.9 %all-to-all-done.2 = bf16[32,6,3584]{2,1,0:T(8,128)(2,1)S(1)} async-done(((bf16[32,6,3584]{2,1,0:T(8,128)(2,1)}), bf16[32,6,3584]{2,1,0:T(8,128)(2,1)S(1)}, u32[]{:S(2)}, u32[]{:S(2)}) %all-to-all-start.2) | async-done | bytes 1376288 | tf_op jit(solution)/shard_map/all_to_all | solution.py:41
  275.3 6.1 %convolution_convert_fusion = bf16[3584,1024]{1,0:T(8,128)(2,1)} fusion(bf16[192,3584]{1,0:T(8,128)(2,1)S(1)} %reshape.59, bf16[1,192,1024]{2,1,0:T(8,128)(2,1)} %param.9, f32[192]{0:T(256)S(1)} %reshape.61), kind=kOutput, calls=%fused_computation | convolution fusion | flops 1413545984 | bytes 9110272 | tf_op jit(solution)/shard_map/dot_general | solution.py:62
  281.5 77.7 %reduce-scatter.2.cloned.1.call-done = bf16[896,1024]{1,0:T(8,128)(2,1)} async-done(((bf16[3584,1024]{1,0:T(8,128)(2,1)}), bf16[896,1024]{1,0:T(8,128)(2,1)}) %reduce-scatter.2.cloned.1.call-update) | async-done | bytes 1835024 | tf_op jit(solution)/shard_map/reduce_scatter | solution.py:61
  (12 shorter events, 1.0 us)
Async XLA Ops:
  9.2 22.1 %all-to-all-start.3 = ((bf16[8,24,8]{1,2,0:T(8,128)(2,1)}), bf16[8,24,8]{1,2,0:T(8,128)(2,1)S(1)}, u32[]{:S(2)}, u32[]{:S(2)}) async-start(bf16[8,24,8]{1,2,0:T(8,128)(2,1)} %fusion.5), calls=%async_computation.3 | async-start | bytes 32768 | tf_op jit(solution)/shard_map/all_to_all | solution.py:26
  31.3 8.6 %all-to-all-start = ((s32[8,1,192]{2,1,0:T(1,128)}), s32[8,1,192]{2,1,0:T(1,128)S(1)}, u32[]{:S(2)}, u32[]{:S(2)}) async-start(s32[8,1,192]{2,1,0:T(1,128)} %reshape.69), calls=%async_computation | async-start | bytes 16384 | tf_op jit(solution)/shard_map/all_to_all | solution.py:25
  39.9 22.8 %all-to-all-start.1 = ((bf16[8,24,3584]{2,1,0:T(8,128)(2,1)}), bf16[8,24,3584]{2,1,0:T(8,128)(2,1)S(1)}, u32[]{:S(2)}, u32[]{:S(2)}) async-start(bf16[8,24,3584]{2,1,0:T(8,128)(2,1)} %broadcast_select_fusion), calls=%async_computation.1 | async-start | bytes 2752512 | tf_op jit(solution)/shard_map/all_to_all | solution.py:24
  62.7 38.1 %all-to-all-start.4 = ((bf16[32,1,6]{2,1,0:T(2,128)(2,1)}), bf16[32,1,6]{2,1,0:T(2,128)(2,1)S(1)}, u32[]{:S(2)}, u32[]{:S(2)}) async-start(bf16[32,1,6]{2,1,0:T(2,128)(2,1)} %convert_element_type.65), calls=%async_computation.4 | async-start | bytes 32768 | tf_op jit(solution)/shard_map/all_to_all | solution.py:48
  100.8 174.1 %all-to-all-start.2 = ((bf16[32,6,3584]{2,1,0:T(8,128)(2,1)}), bf16[32,6,3584]{2,1,0:T(8,128)(2,1)S(1)}, u32[]{:S(2)}, u32[]{:S(2)}) async-start(bf16[32,6,3584]{2,1,0:T(8,128)(2,1)} %reshape.58), calls=%async_computation.2 | async-start | bytes 3670016 | tf_op jit(solution)/shard_map/all_to_all | solution.py:41
  104.8 254.4 %reduce-scatter.2.cloned.1.call-start = ((), (), s32[]{:S(2)}) async-start(), calls=%async_computation.6 | async-start | bytes 9175040 | tf_op jit(solution)/shard_map/reduce_scatter | solution.py:61
Sparse Core Ops, SparseCore 0:
  281.6 77.5 reduce-scatter.1
where the time goes:
time: 367 us; the launch traced here: 366 us
  waiting for transfers between devices  288 us (78%)
  starting transfers between devices  46.4 us (13%)
  between operations  13.5 us (4%)
  other arithmetic  7.25 us (2%)
  matrix products  6.65 us (2%)
  local copies, waits for them, and re-layouts  4.29 us (1%)
    all_to_all x1, waiting for transfers between devices, shards(): lax.all_to_all(bucket.reshape(local_count, block_slots, features), 'local...  170 us
    reduce_scatter x1, waiting for transfers between devices, shards(): lax.psum_scatter(lax.dot_general(expert_rows, scaled, (((0,), (0,)), ((),...  77.7 us
    all_to_all x1, waiting for transfers between devices, shards(): lax.all_to_all(bucket_gates.reshape(local_count, block_slots), 'local', s...  19.3 us
    all_to_all x1, starting transfers between devices, shards(): lax.all_to_all(gates_out, 'node', split_axis=0, concat_axis=0, tiled=True)  17.4 us
    all_to_all x1, starting transfers between devices, shards(): lax.all_to_all(bucket_gates.reshape(local_count, block_slots), 'local', s...  16.8 us
    all_to_all x1, waiting for transfers between devices, shards(): lax.all_to_all(outgoing, 'node', split_axis=0, concat_axis=0, tiled=True)  14.8 us
  transfers between devices with their start and end apart: 6, of which 6 were waited for; matrix products, arithmetic and copies ran while one was open for 2% of the time, Pallas kernels for 0%

commit v1 on v0

v1 whole, which is shorter than its diff:
```python
import jax
import jax.numpy as jnp
from jax import lax
from jax.experimental import pallas as pl
from jax.experimental.pallas import tpu as pltpu
from jax.sharding import PartitionSpec as P

MESH = pl.DeviceIdType.MESH
LANES = 128
TOK_PAD = 32
META = 32
CHUNKS = 2


def remote(src, dst, send_sem, recv_sem, **device):
    return pltpu.make_async_remote_copy(
        src_ref=src,
        dst_ref=dst,
        send_sem=send_sem,
        recv_sem=recv_sem,
        device_id=device,
        device_id_type=MESH,
    )


def kernel(
    rows_ref,
    ids_ref,
    slots_ref,
    gates_ref,
    hidden_ref,
    out_ref,
    ystage,
    yrecv,
    zbuf,
    near,
    far,
    far_in,
    relay_in,
    direct_in,
    bucket,
    hid_all,
    hid_perm,
    acc,
    y_send,
    y_recv,
    h_send,
    h_recv,
    h_local,
    z_send,
    z_recv,
    f_send,
    f_recv,
    r_send,
    r_recv,
    d_send,
    d_recv,
):
    bf16, f32 = jnp.bfloat16, jnp.float32
    node, z, y = lax.axis_index("node"), lax.axis_index("local"), lax.axis_index("dp")
    n_z, n_y = lax.axis_size("local"), lax.axis_size("dp")
    n_x = lax.axis_size("node") // 2
    x, core = node // 2, lax.rem(node, 2)
    sibling = x * 2 + (1 - core)
    x_up, x_down = lax.rem(x + 1, n_x), lax.rem(x + n_x - 1, n_x)
    z_up, z_down = lax.rem(z + 1, n_z), lax.rem(z + n_z - 1, n_z)
    n_tok = rows_ref.shape[0]
    half = n_z // 2
    feats = out_ref.shape[0]
    n_col = feats // LANES
    tokens = n_y * n_tok
    data_rows = n_col * tokens
    chunk = (data_rows + META) // CHUNKS
    slots = hidden_ref.shape[0] // n_z
    per_block = n_y * slots
    pair = 2 * per_block
    top = ids_ref.shape[1]

    barrier = pltpu.get_barrier_semaphore()
    greet = [{"dp": lax.rem(y + d, n_y)} for d in range(1, n_y)]
    greet += [{"local": z_up}, {"local": z_down}, {"node": sibling}]
    greet += [{"node": x_up * 2 + core}, {"node": x_down * 2 + core}]
    for device in greet:
        pl.semaphore_signal(barrier, inc=1, device_id=device, device_id_type=MESH)

    ystage[...] = jnp.zeros_like(ystage)
    put = (
        lax.broadcasted_iota(jnp.int32, (n_tok, LANES), 1)
        == lax.broadcasted_iota(jnp.int32, (n_tok, LANES), 0) + y * n_tok
    ).astype(bf16)

    def on_lanes(values):
        return lax.dot_general(
            values.astype(f32).astype(bf16),
            put,
            (((0,), (0,)), ((), ())),
            preferred_element_type=f32,
        )

    slot_values = slots_ref[...]
    position = jnp.where(slot_values >= 0, slot_values + y * slots, 31)
    meta = jnp.concatenate(
        [
            on_lanes(ids_ref[...]),
            on_lanes(position),
            on_lanes(gates_ref[...]),
            jnp.zeros((META - 3 * top, LANES), f32),
        ],
        axis=0,
    ).astype(bf16)
    for part in range(n_y):
        ystage[part, :n_tok, :feats] = rows_ref[:, part * feats : (part + 1) * feats]
        ystage[part, :, feats:] = meta

    pl.semaphore_wait(barrier, len(greet))

    def y_copy(d):
        peer = lax.rem(y + d, n_y)
        return remote(
            ystage.at[peer], yrecv.at[y], y_send.at[d - 1], y_recv.at[d - 1], dp=peer
        )

    for d in range(1, n_y):
        y_copy(d).start()
    yrecv[y] = ystage[y]

    def y_arrival(d):
        sender = lax.rem(y + n_y - d, n_y)
        return remote(
            ystage.at[sender], yrecv.at[sender], y_send.at[d - 1], y_recv.at[d - 1], dp=sender
        )

    for d in range(1, n_y):
        y_arrival(d).wait_recv()

    to = lax.broadcasted_iota(jnp.int32, (tokens, n_y * TOK_PAD), 0)
    of = lax.broadcasted_iota(jnp.int32, (tokens, n_y * TOK_PAD), 1)
    pick = jnp.zeros((tokens, n_y * TOK_PAD), jnp.bool_)
    for part in range(n_y):
        pick = pick | (
            (of - part * TOK_PAD == to - part * n_tok)
            & (of >= part * TOK_PAD)
            & (of < part * TOK_PAD + n_tok)
        )
    arrived = yrecv[...].reshape(n_y * TOK_PAD, feats + LANES)
    block = jnp.dot(
        pick.astype(bf16), arrived[:, :feats], preferred_element_type=f32
    ).astype(bf16)
    for j in range(n_col):
        zbuf[0, 0, j * tokens : (j + 1) * tokens, :] = block[:, j * LANES : (j + 1) * LANES]
    total = yrecv[0, :, feats:].astype(f32)
    for part in range(1, n_y):
        total = total + yrecv[part, :, feats:].astype(f32)
    zbuf[0, 0, data_rows:, :] = total.astype(bf16)

    def z_copy(side, slot, to_side, to_slot, c):
        piece = pl.ds(c * chunk, chunk)
        return remote(
            zbuf.at[side, slot, piece],
            zbuf.at[to_side, to_slot, piece],
            z_send.at[side, slot, c],
            z_recv.at[to_side, to_slot, c],
            local=z_up if side == 0 else z_down,
        )

    def z_own(side, c):
        piece = pl.ds(c * chunk, chunk)
        return remote(
            zbuf.at[0, 0, piece],
            zbuf.at[side, 1, piece],
            z_send.at[side, 0, c],
            z_recv.at[side, 1, c],
            local=z_up if side == 0 else z_down,
        )

    for c in range(CHUNKS):
        for side in range(2):
            z_own(side, c).start()

    def h_copy(d):
        peer = lax.rem(y + d, n_y)
        return remote(
            hidden_ref, hid_all.at[y], h_send.at[d - 1], h_recv.at[d - 1], dp=peer
        )

    def h_arrival(d):
        sender = lax.rem(y + n_y - d, n_y)
        return remote(
            hidden_ref, hid_all.at[sender], h_send.at[d - 1], h_recv.at[d - 1], dp=sender
        )

    for d in range(1, n_y):
        h_copy(d).start()
    own_hidden = pltpu.make_async_copy(hidden_ref, hid_all.at[y], h_local)
    own_hidden.start()

    def far_copy(b):
        return remote(far.at[b], far_in.at[b], f_send.at[b], f_recv.at[b], node=sibling)

    def direction(b):
        up = lax.rem(b, 2) == 0
        return jnp.where(up, x_up, x_down), jnp.where(up, x_down, x_up)

    def relay_copy(b):
        ahead, _ = direction(b)
        opposite = lax.rem(x + 2, n_x)
        return remote(
            near.at[b, opposite],
            relay_in.at[b],
            r_send.at[b],
            r_recv.at[b],
            node=ahead * 2 + core,
        )

    def direct_copy(b, target, lane):
        return remote(
            near.at[b, target],
            direct_in.at[b, lane],
            d_send.at[b, lane],
            d_recv.at[b, lane],
            node=target * 2 + core,
        )

    def lanes_of(b):
        up = lax.rem(b, 2) == 0
        return jnp.where(up, 0, 1), jnp.where(up, 1, 0)

    row = lax.broadcasted_iota(jnp.int32, (n_x, per_block, LANES), 0)
    place_in = lax.broadcasted_iota(jnp.int32, (n_x, per_block, LANES), 1)

    def place(t):
        slot = lax.rem(t, half)
        b = t - 1
        codes, gates = [], []
        sides = []
        for side in range(2):
            routing = zbuf[side, slot, data_rows:, :].astype(f32)
            codes.append(routing[:top] * 32.0 + routing[top : 2 * top])
            gates.append(routing[2 * top : 3 * top])
            sides += [
                jnp.concatenate(
                    [
                        zbuf[side, slot, j * tokens : (j + 1) * tokens, :]
                        for j in range(n_col)
                    ],
                    axis=1,
                ),
                jnp.zeros((LANES - tokens, feats), bf16),
            ]
        values = jnp.concatenate(sides, axis=0)
        for which, dest in ((1 - core, far), (core, near)):
            target = (((row * 2 + which) * n_z + z) * 32 + place_in).astype(f32)
            parts = []
            for side in range(2):
                weight = jnp.zeros((n_x, per_block, LANES), f32)
                for k in range(top):
                    weight = weight + jnp.where(
                        codes[side][k : k + 1, :][None] == target,
                        gates[side][k : k + 1, :][None],
                        0.0,
                    )
                blank = jnp.zeros_like(weight)
                both = (weight, blank) if side == 0 else (blank, weight)
                parts.append(jnp.concatenate(both, axis=1).reshape(n_x * pair, LANES))
            placement = jnp.concatenate(parts, axis=1).astype(bf16)
            placed = jnp.dot(placement, values, preferred_element_type=f32)
            dest[b] = placed.astype(bf16).reshape(n_x, pair, feats)
            if dest is far:
                far_copy(b).start()

    def merge_core(t):
        b = t - 1
        far_copy(b).wait_recv()
        near[b] = near[b] + far_in[b]
        relay_copy(b).start()
        _, behind = direction(b)
        _, lane = lanes_of(b)
        direct_copy(b, behind, lane).start()

    def merge_relay(t):
        b = t - 1
        relay_copy(b).wait_recv()
        ahead, _ = direction(b)
        lane, _ = lanes_of(b)
        near[b, ahead] = near[b, ahead] + relay_in[b]
        direct_copy(b, ahead, lane).start()

    def finish(t):
        b = t - 1
        direct_copy(b, x_up, 0).wait_recv()
        direct_copy(b, x_down, 1).wait_recv()
        bucket[b] = near[b, x] + direct_in[b, 0] + direct_in[b, 1]

    group_pairs = half // 4
    group = group_pairs * pair

    def order_hidden():
        for d in range(1, n_y):
            h_arrival(d).wait_recv()
        own_hidden.wait()
        wide = (group, n_y * n_z * slots)

        @pl.loop(0, 4)
        def _(g):
            i = lax.broadcasted_iota(jnp.int32, (group, 1), 0)
            step = lax.div(i, pair) + g * group_pairs + 1
            side = lax.rem(lax.div(i, per_block), 2)
            at = lax.rem(i, per_block)
            source = jnp.where(side == 0, z - lax.rem(step, half), z + step)
            source = lax.rem(source + n_z, n_z)
            replica = lax.div(at, slots)
            column = replica * (n_z * slots) + source * slots + (at - replica * slots)
            choose = (lax.broadcasted_iota(jnp.int32, wide, 1) == column).astype(bf16)
            hid_perm[g] = jnp.dot(
                choose,
                hid_all[...].reshape(wide[1], hid_all.shape[2]),
                preferred_element_type=f32,
            ).astype(bf16)

    def product(g, first, last):
        @pl.loop(0, n_col)
        def _(j):
            cols = pl.ds(pl.multiple_of(j * LANES, LANES), LANES)
            left = bucket[g * group_pairs : (g + 1) * group_pairs, :, cols]
            term = lax.dot_general(
                left.reshape(group, LANES),
                hid_perm[g],
                (((0,), (0,)), ((), ())),
                preferred_element_type=f32,
            )
            if not first:
                term = term + acc[cols, :]
            if last:
                out_ref[cols, :] = term.astype(bf16)
            else:
                acc[cols, :] = term

    def z_step(t, c):
        for side in range(2):
            z_copy(side, t - 1, side, t, c).wait_recv()

            @pl.when(t < half - 1)
            def _():
                z_copy(side, t, side, t + 1, c).start()

            if side == c:

                @pl.when(t == half - 1)
                def _():
                    z_copy(side, t, 1, 0, c).start()

    @pl.loop(1, half + 4)
    def _(t):
        @pl.when(t < half)
        def _():
            z_step(t, 0)

        @pl.when((t > 1) & (t <= half + 1))
        def _():
            merge_core(t - 1)

        @pl.when((t > 2) & (t <= half + 2))
        def _():
            merge_relay(t - 2)

        @pl.when(t < half)
        def _():
            z_step(t, 1)

        @pl.when(t == half)
        def _():
            for c in range(CHUNKS):
                z_copy(c, half - 1, 1, 0, c).wait_recv()

        @pl.when(t <= half)
        def _():
            place(t)

        @pl.when(t > 3)
        def _():
            finish(t - 3)

        @pl.when(t == half // 2)
        def _():
            order_hidden()

        for g in range(3):

            @pl.when(t == max(half // 2 + 1, group_pairs * (g + 1) + 3) + (g == 1))
            def _():
                product(g, g == 0, False)

    product(3, False, True)

    for d in range(1, n_y):
        y_copy(d).wait_send()
        h_copy(d).wait_send()
    for c in range(CHUNKS):
        for side in range(2):
            z_own(side, c).wait_send()

            @pl.loop(1, half - 1)
            def _(t):
                z_copy(side, t, side, t + 1, c).wait_send()

        z_copy(c, half - 1, 1, 0, c).wait_send()

    @pl.loop(0, half)
    def _(b):
        far_copy(b).wait_send()
        relay_copy(b).wait_send()
        direct_copy(b, x_up, 0).wait_send()
        direct_copy(b, x_down, 1).wait_send()


def shards(grad_out, expert_ids, slot_ids, gate_values, hidden):
    n_x = lax.axis_size("node") // 2
    n_z, n_y = lax.axis_size("local"), lax.axis_size("dp")
    n_tok, width = grad_out.shape
    _, capacity, units = hidden.shape
    feats = width // n_y
    half = n_z // 2
    pair = 2 * n_y * capacity // n_z
    block_rows = feats // LANES * n_y * n_tok + META
    bf16 = jnp.bfloat16
    vmem = pl.BlockSpec(memory_space=pltpu.VMEM)
    dma = pltpu.SemaphoreType.DMA
    result = pl.pallas_call(
        kernel,
        out_shape=jax.ShapeDtypeStruct((feats, units), bf16),
        in_specs=[vmem] * 4 + [pl.BlockSpec(memory_space=pl.ANY)],
        out_specs=vmem,
        scratch_shapes=[
            pltpu.VMEM((n_y, TOK_PAD, feats + LANES), bf16),
            pltpu.VMEM((n_y, TOK_PAD, feats + LANES), bf16),
            pltpu.VMEM((2, half, block_rows, LANES), bf16),
            pltpu.VMEM((half, n_x, pair, feats), bf16),
            pltpu.VMEM((half, n_x, pair, feats), bf16),
            pltpu.VMEM((half, n_x, pair, feats), bf16),
            pltpu.VMEM((half, pair, feats), bf16),
            pltpu.VMEM((half, 2, pair, feats), bf16),
            pltpu.VMEM((half, pair, feats), bf16),
            pltpu.VMEM((n_y, capacity, units), bf16),
            pltpu.VMEM((4, half // 4 * pair, units), bf16),
            pltpu.VMEM((feats, units), jnp.float32),
            dma((n_y - 1,)),
            dma((n_y - 1,)),
            dma((n_y - 1,)),
            dma((n_y - 1,)),
            dma,
            dma((2, half, CHUNKS)),
            dma((2, half, CHUNKS)),
            dma((half,)),
            dma((half,)),
            dma((half,)),
            dma((half,)),
            dma((half, 2)),
            dma((half, 2)),
        ],
        compiler_params=pltpu.CompilerParams(
            collective_id=0, has_side_effects=True, vmem_limit_bytes=56 * 1024 * 1024
        ),
        cost_estimate=pl.CostEstimate(
            flops=2 * n_y * capacity * feats * units, bytes_accessed=4 << 20, transcendentals=0
        ),
    )(grad_out, expert_ids, slot_ids, gate_values, hidden[0])
    return result[None]


def solution(mesh):
    in_specs = (
        P(("node", "local", "dp"), None),
        P(("node", "local", "dp"), None),
        P(("node", "local", "dp"), None),
        P(("node", "local", "dp"), None),
        P(("node", "local"), "dp", None),
    )
    out_specs = P(("node", "local"), "dp", None)
    return jax.shard_map(shards, mesh=mesh, in_specs=in_specs, out_specs=out_specs, check_vma=False)
```

time: 367 us -> 120 us (0.33)
  waiting for transfers between devices: 288 us -> 0 us
  Pallas kernels: 0 us -> 112 us
  starting transfers between devices: 46.4 us -> 0 us
  between operations: 13.5 us -> 0.01 us
  other arithmetic: 7.25 us -> 0 us
  matrix products: 6.65 us -> 0 us
    all_to_all x5 -> x0, waiting for transfers between devices: 210 us -> none  [the longest x1 170 us: shards(): lax.all_to_all(bucket.reshape(local_count, block_slots, features), 'local...]
    pallas_call x0 -> x1, Pallas kernels: none -> 112 us  [shards(): pl.pallas_call(kernel, out_shape=jax.ShapeDtypeStruct((feats, units), bf1...]
    reduce_scatter x1 -> x0, waiting for transfers between devices: 77.7 us -> none  [shards(): lax.psum_scatter(lax.dot_general(expert_rows, scaled, (((0,), (0,)), ((),...]
    all_to_all x5 -> x0, starting transfers between devices: 46.3 us -> none  [the longest x1 17.4 us: shards(): lax.all_to_all(gates_out, 'node', split_axis=0, concat_axis=0, tiled=True)]
    dot_general x2 -> x0, matrix products: 6.65 us -> none  [the longest x1 6.13 us: shards(): lax.dot_general(expert_rows, scaled, (((0,), (0,)), ((), ())), preferred_...]
    unnamed x2 -> x4, local copies, waits for them, and re-layouts: 0.76 us -> 6.94 us
    select_n x3 -> x0, other arithmetic: 4.17 us -> none  [the longest x1 2.16 us: shards(): jnp.where(chosen[:, :, None], grad_out[None, :, :], jnp.zeros((), jnp.bfl...]
  transfers between devices with their start and end apart: 6 -> 0, of which waited for: 6 -> 0; matrix products, arithmetic and copies ran while one was open for 2% -> 0% of each run, Pallas kernels for 0% -> 0%
where the time goes in v1:
time: 120 us; the launch traced here: 119 us
  Pallas kernels  112 us (93%)
  local copies, waits for them, and re-layouts  6.94 us (6%)
    pallas_call x1, Pallas kernels, shards(): pl.pallas_call(kernel, out_shape=jax.ShapeDtypeStruct((feats, units), bf1...  112 us
    unnamed x4, local copies, waits for them, and re-layouts  6.94 us

profile of v1, /device:TPU:1, one launch (start us, length us, event | category | flops | bytes accessed | tf_op | source)
XLA Modules:
  0.0 119.4 jit_solution(9714391036293019448)
XLA Ops:
  0.0 1.4 %copy.8.gates_ref = bf16[24,8]{1,0:T(8,128)(2,1)} copy(bf16[24,8]{0,1:T(8,128)(2,1)} %param.8) | data formatting | bytes 768 | tf_op args[3]
  1.4 1.4 %copy.6.ids_ref = s32[24,8]{1,0:T(8,128)} copy(s32[24,8]{0,1:T(8,128)} %param.6) | data formatting | bytes 1536 | tf_op args[1]
  2.7 1.4 %copy.7.slots_ref = s32[24,8]{1,0:T(8,128)} copy(s32[24,8]{0,1:T(8,128)} %param.7) | data formatting | bytes 1536 | tf_op args[2]
  4.1 112.4 %shard_map.55 = bf16[896,1024]{1,0:T(8,128)(2,1)} custom-call(bf16[24,3584]{1,0:T(8,128)(2,1)} %rows_ref.1, s32[24,8]{1,0:T(8,128)} %copy.6.ids_ref, s32[24,8]{1,0:T(8,128)} %copy.7.slots_ref, bf16[24,8]{1,0:T(8,128)(2,1)} %copy.8.gates_ref, bf16[192,1024]{1,0:T(8,128)(2,1)} %bitcast.3), custom_call_target="tpu_custom_call" | custom-call | flops 1409286144 | bytes 4194304 | tf_op jit(solution)/shard_map/pallas_call | solution.py:428
  116.5 2.9 %copy.10 = bf16[1,896,1024]{2,1,0:T(8,128)(2,1)} copy(bf16[1,896,1024]{2,1,0:T(8,128)(2,1)} %bitcast.2) | data formatting | bytes 3670016

commit v2 on v1

v2 whole, which is shorter than its diff:
```python
import jax
import jax.numpy as jnp
from jax import lax
from jax.experimental import pallas as pl
from jax.experimental.pallas import tpu as pltpu
from jax.sharding import PartitionSpec as P

MESH = pl.DeviceIdType.MESH
LANES = 128
CODE = 32
ONE = 32
GROUPS = 3


def remote(src, dst, send_sem, recv_sem, **device):
    return pltpu.make_async_remote_copy(
        src_ref=src,
        dst_ref=dst,
        send_sem=send_sem,
        recv_sem=recv_sem,
        device_id=device,
        device_id_type=MESH,
    )


def kernel(
    rows_ref,
    ids_ref,
    slots_ref,
    gates_ref,
    hidden_ref,
    out_ref,
    stage,
    zbuf,
    near,
    far,
    far_in,
    relay_in,
    direct_in,
    near_one,
    far_one,
    far_one_in,
    direct_one_in,
    bucket,
    bucket_one,
    hid_all,
    hid_perm,
    hid_one,
    acc,
    y_send,
    y_recv,
    h_send,
    h_recv,
    h_local,
    z_send,
    z_recv,
    f_send,
    f_recv,
    r_send,
    r_recv,
    d_send,
    d_recv,
    e_send,
    e_recv,
):
    bf16, f32 = jnp.bfloat16, jnp.float32
    node, z, y = lax.axis_index("node"), lax.axis_index("local"), lax.axis_index("dp")
    n_z, n_y = lax.axis_size("local"), lax.axis_size("dp")
    n_x = lax.axis_size("node") // 2
    x, core = node // 2, lax.rem(node, 2)
    sibling = x * 2 + (1 - core)
    x_up, x_down = lax.rem(x + 1, n_x), lax.rem(x + n_x - 1, n_x)
    z_up, z_down = lax.rem(z + 1, n_z), lax.rem(z + n_z - 1, n_z)
    n_tok = rows_ref.shape[0]
    half = n_z // 2
    last = half - 1
    feats = out_ref.shape[0]
    n_col = feats // LANES
    top = ids_ref.shape[0]
    data_rows = n_col * n_tok
    piece = data_rows + top
    lane_group = LANES // n_y
    slots = hidden_ref.shape[0] // n_z
    per_block = n_y * slots
    pair = 2 * per_block

    barrier = pltpu.get_barrier_semaphore()
    opposite = lax.rem(x + 2, n_x)
    greet = [{"dp": lax.rem(y + d, n_y)} for d in range(1, n_y)]
    greet += [{"local": z_up}, {"local": z_down}, {"node": sibling}]
    greet += [{"node": chip * 2 + core} for chip in (x_up, x_down, opposite)]
    for device in greet:
        pl.semaphore_signal(barrier, inc=1, device_id=device, device_id_type=MESH)

    def on_lanes(values, group):
        put = lax.broadcasted_iota(jnp.int32, (n_tok, LANES), 1) == (
            lax.broadcasted_iota(jnp.int32, (n_tok, LANES), 0) + group * lane_group
        )
        return jnp.dot(
            values.astype(f32).astype(bf16), put.astype(bf16), preferred_element_type=f32
        )

    slot_values = slots_ref[...]
    position = jnp.where(slot_values >= 0, slot_values + y * slots, CODE - 1)
    routing = on_lanes(ids_ref[...], 0) + on_lanes(position, 1) + on_lanes(gates_ref[...], 2)

    def piece_rows(k):
        return pl.ds(k * piece, piece)

    for d in range(n_y):
        k = (n_y - d) % n_y
        peer = lax.rem(y + d, n_y)
        columns = [
            rows_ref[:, pl.ds(pl.multiple_of(peer * feats + j * LANES, LANES), LANES)].astype(f32)
            for j in range(n_col)
        ]
        columns.append(pltpu.roll(routing, k * lane_group, 1) if k else routing)
        whole = jnp.concatenate(columns, axis=0).astype(bf16)
        if d == 0:
            zbuf[0, 0, :piece, :] = whole
        else:
            stage[d - 1] = whole

    pl.semaphore_wait(barrier, len(greet))

    def y_copy(d):
        return remote(
            stage.at[d - 1],
            zbuf.at[0, 0, piece_rows(n_y - d)],
            y_send.at[d - 1],
            y_recv.at[d - 1],
            dp=lax.rem(y + d, n_y),
        )

    def z_copy(side, slot, to_side, to_slot, k):
        return remote(
            zbuf.at[side, slot, piece_rows(k)],
            zbuf.at[to_side, to_slot, piece_rows(k)],
            z_send.at[side, slot, k],
            z_recv.at[to_side, to_slot, k],
            local=z_up if side == 0 else z_down,
        )

    def z_own(side, k):
        return remote(
            zbuf.at[0, 0, piece_rows(k)],
            zbuf.at[side, 1, piece_rows(k)],
            z_send.at[side, 0, k],
            z_recv.at[side, 1, k],
            local=z_up if side == 0 else z_down,
        )

    for d in (1, n_y - 1, 2):
        y_copy(d).start()
    for side in range(2):
        z_own(side, 0).start()
    y_copy(n_y - 1).wait_recv()
    z_own(0, 1).start()
    y_copy(1).wait_recv()
    z_own(1, 3).start()
    z_own(0, 3).start()
    y_copy(2).wait_recv()
    z_own(1, 2).start()
    z_own(0, 2).start()
    z_own(1, 1).start()
    order = ((0, 1, 3, 2), (0, 3, 2, 1))
    to_opposite = ((0, 1), (3, 2))

    def h_copy(d):
        return remote(
            hidden_ref,
            hid_all.at[y],
            h_send.at[d - 1],
            h_recv.at[d - 1],
            dp=lax.rem(y + d, n_y),
        )

    def h_arrival(d):
        sender = lax.rem(y + n_y - d, n_y)
        return remote(
            hidden_ref, hid_all.at[sender], h_send.at[d - 1], h_recv.at[d - 1], dp=sender
        )

    for d in range(1, n_y):
        h_copy(d).start()
    own_hidden = pltpu.make_async_copy(hidden_ref, hid_all.at[y], h_local)
    own_hidden.start()

    def far_copy(b):
        return remote(far.at[b], far_in.at[b], f_send.at[b], f_recv.at[b], node=sibling)

    def far_one_copy(s):
        return remote(
            far_one.at[s],
            far_one_in.at[s],
            f_send.at[last + s],
            f_recv.at[last + s],
            node=sibling,
        )

    cut = (n_col + 1) // 2 * LANES
    ways = ((x_up, slice(0, cut)), (x_down, slice(cut, feats)))

    def relay_copy(b, way):
        ahead, cols = ways[way]
        return remote(
            near.at[b, opposite, :, cols],
            relay_in.at[b, :, cols],
            r_send.at[b, way],
            r_recv.at[b, way],
            node=ahead * 2 + core,
        )

    def direct_copy(b, way):
        ahead, _ = ways[way]
        return remote(
            near.at[b, ahead],
            direct_in.at[b, way],
            d_send.at[b, way],
            d_recv.at[b, way],
            node=ahead * 2 + core,
        )

    def direct_one_copy(s, way):
        chip = (x_up, x_down, opposite)[way]
        return remote(
            near_one.at[s, chip],
            direct_one_in.at[s, way],
            e_send.at[s, way],
            e_recv.at[s, way],
            node=chip * 2 + core,
        )

    row = lax.broadcasted_iota(jnp.int32, (n_x, per_block, LANES), 0)
    place_in = lax.broadcasted_iota(jnp.int32, (n_x, per_block, LANES), 1)
    lane_of = lax.broadcasted_iota(jnp.int32, (top, LANES), 1) // lane_group

    def read_block(side, slot):
        block = zbuf[side, slot].astype(f32)
        gap = jnp.zeros((lane_group - n_tok, LANES), f32)
        columns = []
        for j in range(n_col):
            rows = []
            for k in range(n_y):
                start = k * piece + j * n_tok
                rows += [block[start : start + n_tok], gap]
            columns.append(jnp.concatenate(rows, axis=0))
        values = jnp.concatenate(columns, axis=1).astype(bf16)
        parts = []
        for shift in range(3):
            part = jnp.zeros((top, LANES), f32)
            for k in range(n_y):
                held = block[k * piece + data_rows : (k + 1) * piece]
                part = jnp.where(lane_of == (k + shift) % n_y, held, part)
            parts.append(
                pltpu.roll(part, LANES - shift * lane_group, 1) if shift else part
            )
        return values, parts[0] * float(CODE) + parts[1], parts[2]

    def weights(codes, gates, which):
        target = (((row * 2 + which) * n_z + z) * CODE + place_in).astype(f32)
        weight = jnp.zeros((n_x, per_block, LANES), f32)
        for k in range(top):
            weight = weight + jnp.where(
                codes[k : k + 1, :][None] == target, gates[k : k + 1, :][None], 0.0
            )
        return weight

    def place(t):
        b = t - 1
        blocks = [read_block(side, t) for side in range(2)]
        values = jnp.concatenate([values for values, _, _ in blocks], axis=0)
        for which, dest in ((1 - core, far), (core, near)):
            parts = []
            for side in range(2):
                weight = weights(*blocks[side][1:], which)
                blank = jnp.zeros_like(weight)
                both = (weight, blank) if side == 0 else (blank, weight)
                parts.append(jnp.concatenate(both, axis=1).reshape(n_x * pair, LANES))
            placement = jnp.concatenate(parts, axis=1).astype(bf16)
            placed = jnp.dot(placement, values, preferred_element_type=f32)
            dest[b] = placed.astype(bf16).reshape(n_x, pair, feats)
            if dest is far:
                far_copy(b).start()

    def place_one(s):
        values, codes, gates = read_block(s, 0)
        gap = jnp.zeros((n_x, ONE - per_block, LANES), f32)
        for which, dest in ((1 - core, far_one), (core, near_one)):
            weight = jnp.concatenate([weights(codes, gates, which), gap], axis=1)
            placed = jnp.dot(
                weight.reshape(n_x * ONE, LANES).astype(bf16),
                values,
                preferred_element_type=f32,
            )
            dest[s] = placed.astype(bf16).reshape(n_x, ONE, feats)
            if dest is far_one:
                far_one_copy(s).start()

    def merge_core(t):
        b = t - 1
        far_copy(b).wait_recv()
        near[b, opposite] = near[b, opposite] + far_in[b, opposite]
        for way in range(2):
            relay_copy(b, way).start()
        for chip in (x_up, x_down, x):
            near[b, chip] = near[b, chip] + far_in[b, chip]

    def merge_relay(t):
        b = t - 1
        for way in range(2):
            ahead, cols = ways[way]
            relay_copy(b, way).wait_recv()
            near[b, ahead, :, cols] = near[b, ahead, :, cols] + relay_in[b, :, cols]
            direct_copy(b, way).start()

    def finish(t):
        b = t - 1
        for way in range(2):
            direct_copy(b, way).wait_recv()
        bucket[b] = near[b, x] + direct_in[b, 0] + direct_in[b, 1]

    def merge_one(s):
        far_one_copy(s).wait_recv()
        for way, chip in ((2, opposite), (0, x_up), (1, x_down)):
            near_one[s, chip] = near_one[s, chip] + far_one_in[s, chip]
            direct_one_copy(s, way).start()
        near_one[s, x] = near_one[s, x] + far_one_in[s, x]

    def finish_one(s):
        total = near_one[s, x]
        for way in range(3):
            direct_one_copy(s, way).wait_recv()
            total = total + direct_one_in[s, way]
        bucket_one[s] = total

    group_pairs = last // GROUPS
    group = group_pairs * pair
    positions = n_y * n_z * slots

    def choose(count, source, at):
        replica = lax.div(at, slots)
        column = replica * (n_z * slots) + source * slots + (at - replica * slots)
        pick = lax.broadcasted_iota(jnp.int32, (count, positions), 1) == column
        return jnp.dot(
            pick.astype(bf16),
            hid_all[...].reshape(positions, hid_all.shape[2]),
            preferred_element_type=f32,
        ).astype(bf16)

    def order_hidden():
        for d in range(1, n_y):
            h_arrival(d).wait_recv()
        own_hidden.wait()

        @pl.loop(0, GROUPS)
        def _(g):
            i = lax.broadcasted_iota(jnp.int32, (group, 1), 0)
            step = lax.div(i, pair) + g * group_pairs + 1
            side = lax.rem(lax.div(i, per_block), 2)
            source = lax.rem(jnp.where(side == 0, z - step, z + step) + n_z, n_z)
            hid_perm[g] = choose(group, source, lax.rem(i, per_block))

        i = lax.broadcasted_iota(jnp.int32, (2 * ONE, 1), 0)
        source = lax.rem(z + jnp.where(i < ONE, 0, half), n_z)
        at = jnp.where(i < ONE, i, i - ONE)
        hid_one[...] = choose(2 * ONE, source, jnp.where(at < per_block, at, positions))

    def product(g):
        @pl.loop(0, n_col)
        def _(j):
            cols = pl.ds(pl.multiple_of(j * LANES, LANES), LANES)
            if g < GROUPS:
                left = bucket[g * group_pairs : (g + 1) * group_pairs, :, cols]
                left, right = left.reshape(group, LANES), hid_perm[g]
            else:
                left, right = bucket_one[:, :, cols].reshape(2 * ONE, LANES), hid_one[...]
            term = lax.dot_general(
                left, right, (((0,), (0,)), ((), ())), preferred_element_type=f32
            )
            if g > 0:
                term = term + acc[cols, :]
            if g < GROUPS:
                acc[cols, :] = term
            else:
                out_ref[cols, :] = term.astype(bf16)

    place_one(0)

    @pl.loop(1, half)
    def _(t):
        def z_step(at):
            for side in range(2):
                k = order[side][at]
                z_copy(side, t - 1, side, t, k).wait_recv()

                @pl.when(t < last)
                def _():
                    z_copy(side, t, side, t + 1, k).start()

                if k in to_opposite[side]:

                    @pl.when(t == last)
                    def _():
                        z_copy(side, t, 1, 0, k).start()

        z_step(0)
        z_step(1)

        @pl.when(t == 1)
        def _():
            merge_one(0)

        @pl.when(t > 1)
        def _():
            merge_core(t - 1)

        @pl.when(t > 2)
        def _():
            merge_relay(t - 2)

        z_step(2)
        z_step(3)
        place(t)

        @pl.when(t == 3)
        def _():
            finish_one(0)

        @pl.when(t > 3)
        def _():
            finish(t - 3)

        @pl.when(t == half // 2)
        def _():
            order_hidden()

        for g in range(GROUPS - 1):

            @pl.when(t == max(half // 2 + 1, group_pairs * (g + 1) + 3))
            def _():
                product(g)

    merge_core(last)
    merge_relay(last - 1)
    finish(last - 2)
    for side in range(2):
        for k in to_opposite[side]:
            z_copy(side, last, 1, 0, k).wait_recv()
    place_one(1)
    merge_relay(last)
    merge_one(1)
    finish(last - 1)
    finish(last)
    product(GROUPS - 1)
    finish_one(1)
    product(GROUPS)

    for d in range(1, n_y):
        y_copy(d).wait_send()
        h_copy(d).wait_send()
    for k in range(n_y):
        for side in range(2):
            z_own(side, k).wait_send()

            @pl.loop(1, last)
            def _(t):
                z_copy(side, t, side, t + 1, k).wait_send()

            if k in to_opposite[side]:
                z_copy(side, last, 1, 0, k).wait_send()

    @pl.loop(0, last)
    def _(b):
        far_copy(b).wait_send()
        for way in range(2):
            relay_copy(b, way).wait_send()
            direct_copy(b, way).wait_send()

    for s in range(2):
        far_one_copy(s).wait_send()
        for way in range(3):
            direct_one_copy(s, way).wait_send()


def shards(grad_out, expert_ids, slot_ids, gate_values, hidden):
    n_x = lax.axis_size("node") // 2
    n_z, n_y = lax.axis_size("local"), lax.axis_size("dp")
    n_tok, width = grad_out.shape
    top = expert_ids.shape[1]
    _, capacity, units = hidden.shape
    feats = width // n_y
    half = n_z // 2
    last = half - 1
    pair = 2 * n_y * capacity // n_z
    piece = feats // LANES * n_tok + top
    bf16 = jnp.bfloat16
    vmem = pl.BlockSpec(memory_space=pltpu.VMEM)
    dma = pltpu.SemaphoreType.DMA
    result = pl.pallas_call(
        kernel,
        out_shape=jax.ShapeDtypeStruct((feats, units), bf16),
        in_specs=[vmem] * 4 + [pl.BlockSpec(memory_space=pl.ANY)],
        out_specs=vmem,
        scratch_shapes=[
            pltpu.VMEM((n_y - 1, piece, LANES), bf16),
            pltpu.VMEM((2, half, n_y * piece, LANES), bf16),
            pltpu.VMEM((last, n_x, pair, feats), bf16),
            pltpu.VMEM((last, n_x, pair, feats), bf16),
            pltpu.VMEM((last, n_x, pair, feats), bf16),
            pltpu.VMEM((last, pair, feats), bf16),
            pltpu.VMEM((last, 2, pair, feats), bf16),
            pltpu.VMEM((2, n_x, ONE, feats), bf16),
            pltpu.VMEM((2, n_x, ONE, feats), bf16),
            pltpu.VMEM((2, n_x, ONE, feats), bf16),
            pltpu.VMEM((2, 3, ONE, feats), bf16),
            pltpu.VMEM((last, pair, feats), bf16),
            pltpu.VMEM((2, ONE, feats), bf16),
            pltpu.VMEM((n_y, capacity, units), bf16),
            pltpu.VMEM((GROUPS, last // GROUPS * pair, units), bf16),
            pltpu.VMEM((2 * ONE, units), bf16),
            pltpu.VMEM((feats, units), jnp.float32),
            dma((n_y - 1,)),
            dma((n_y - 1,)),
            dma((n_y - 1,)),
            dma((n_y - 1,)),
            dma,
            dma((2, half, n_y)),
            dma((2, half, n_y)),
            dma((last + 2,)),
            dma((last + 2,)),
            dma((last, 2)),
            dma((last, 2)),
            dma((last, 2)),
            dma((last, 2)),
            dma((2, 3)),
            dma((2, 3)),
        ],
        compiler_params=pltpu.CompilerParams(
            collective_id=0, has_side_effects=True, vmem_limit_bytes=56 * 1024 * 1024
        ),
        cost_estimate=pl.CostEstimate(
            flops=2 * n_y * capacity * feats * units, bytes_accessed=4 << 20, transcendentals=0
        ),
    )(grad_out, expert_ids.T, slot_ids.T, gate_values.T, hidden[0])
    return result[None]


def solution(mesh):
    in_specs = (
        P(("node", "local", "dp"), None),
        P(("node", "local", "dp"), None),
        P(("node", "local", "dp"), None),
        P(("node", "local", "dp"), None),
        P(("node", "local"), "dp", None),
    )
    out_specs = P(("node", "local"), "dp", None)
    return jax.shard_map(shards, mesh=mesh, in_specs=in_specs, out_specs=out_specs, check_vma=False)
```

time: 120 us -> 109 us (0.908)
  Pallas kernels: 112 us -> 106 us
  local copies, waits for them, and re-layouts: 6.94 us -> 2.87 us
    pallas_call x1, Pallas kernels: 112 us -> 106 us  [shards(): pl.pallas_call(kernel, out_shape=jax.ShapeDtypeStruct((feats, units), bf1...]
    unnamed x4 -> x1, local copies, waits for them, and re-layouts: 6.94 us -> 2.87 us
where the time goes in v2:
time: 109 us
  Pallas kernels  106 us (97%)
  local copies, waits for them, and re-layouts  2.87 us (3%)
    pallas_call x1, Pallas kernels, shards(): pl.pallas_call(kernel, out_shape=jax.ShapeDtypeStruct((feats, units), bf1...  106 us
    unnamed x1, local copies, waits for them, and re-layouts  2.87 us

profile of v2, /device:TPU:1, one launch (start us, length us, event | category | flops | bytes accessed | tf_op | source)
XLA Modules:
  0.0 109.1 jit_solution(7522874211124492307)
XLA Ops:
  0.0 106.2 %shard_map.55 = bf16[896,1024]{1,0:T(8,128)(2,1)} custom-call(bf16[24,3584]{1,0:T(8,128)(2,1)} %rows_ref.1, s32[8,24]{1,0:T(8,128)} %bitcast.7, s32[8,24]{1,0:T(8,128)} %bitcast.8, bf16[8,24]{1,0:T(8,128)(2,1)} %bitcast.9, bf16[192,1024]{1,0:T(8,128)(2,1)} %bitcast.6), custom_call_target="tpu_custom_call" | custom-call | flops 1409286144 | bytes 4194304 | tf_op jit(solution)/shard_map/pallas_call | solution.py:500
  106.2 2.9 %copy.7 = bf16[1,896,1024]{2,1,0:T(8,128)(2,1)} copy(bf16[1,896,1024]{2,1,0:T(8,128)(2,1)} %bitcast.5) | data formatting | bytes 3670016

commit v3 on v2

v3 whole, which is shorter than its diff:
```python
import jax
import jax.numpy as jnp
from jax import lax
from jax.experimental import pallas as pl
from jax.experimental.pallas import tpu as pltpu
from jax.sharding import PartitionSpec as P

MESH = pl.DeviceIdType.MESH
LANES = 128
CODE = 8
UNIT = 16
SMALL = 8
GROUP = 4
AHEAD = 3
JUMPS = ((2, AHEAD), (0, 2), (1, 2), (0, 1), (1, 1))


def remote(src, dst, send_sem, recv_sem, **device):
    return pltpu.make_async_remote_copy(
        src_ref=src,
        dst_ref=dst,
        send_sem=send_sem,
        recv_sem=recv_sem,
        device_id=device,
        device_id_type=MESH,
    )


def kernel(
    rows_ref,
    ids_ref,
    slots_ref,
    gates_ref,
    hidden_ref,
    out_ref,
    stage,
    held,
    zbuf,
    near,
    far,
    far_in,
    far_jump,
    far_jump_in,
    near_jump,
    jump_in,
    bucket,
    bucket_jump,
    hid_all,
    hid_perm,
    acc,
    y_send,
    y_recv,
    x_send,
    x_recv,
    h_send,
    h_recv,
    h_local,
    z_send,
    z_recv,
    f_send,
    f_recv,
    d_send,
    d_recv,
    g_send,
    g_recv,
    j_send,
    j_recv,
):
    bf16, f32 = jnp.bfloat16, jnp.float32
    node, z, y = lax.axis_index("node"), lax.axis_index("local"), lax.axis_index("dp")
    n_z, n_y = lax.axis_size("local"), lax.axis_size("dp")
    n_x = lax.axis_size("node") // 2
    x, core = node // 2, lax.rem(node, 2)
    sibling = x * 2 + (1 - core)
    z_up, z_down = lax.rem(z + 1, n_z), lax.rem(z + n_z - 1, n_z)
    n_tok = rows_ref.shape[0]
    half = n_z // 2
    raw = half - AHEAD
    n_unit = raw + 1
    feats = out_ref.shape[0]
    n_col = feats // LANES
    top = ids_ref.shape[0]
    data_rows = n_col * n_tok
    piece = data_rows + top
    lane_group = LANES // n_y
    slots = hidden_ref.shape[0] // n_z
    barrier = pltpu.get_barrier_semaphore()
    greet = [{"dp": lax.rem(y + d, n_y)} for d in range(1, n_y)]
    greet += [{"node": sibling}]
    greet += [
        {"node": lax.rem(x + j, n_x) * 2 + core, "local": lax.rem(z + n_z + step, n_z)}
        for step in (1, -1, 2, -2, AHEAD, -AHEAD)
        for j in range(n_x)
    ]
    greet += [{"node": lax.rem(x + j, n_x) * 2 + core} for j in range(1, n_x)]
    for device in greet:
        pl.semaphore_signal(barrier, inc=1, device_id=device, device_id_type=MESH)

    own_group = lax.rem(x + n_y - y, n_x)

    def on_lanes(values, shift):
        start = lax.rem(own_group + shift, n_x) * lane_group
        put = lax.broadcasted_iota(jnp.int32, (n_tok, LANES), 1) == (
            lax.broadcasted_iota(jnp.int32, (n_tok, LANES), 0) + start
        )
        return jnp.dot(
            values.astype(f32).astype(bf16),
            put.astype(f32).astype(bf16),
            preferred_element_type=f32,
        )

    slot_values = slots_ref[...]
    position = jnp.where(slot_values >= 0, slot_values, CODE - 1)
    routing = on_lanes(ids_ref[...], 0) + on_lanes(position, 1) + on_lanes(gates_ref[...], 2)

    def piece_rows(k):
        return pl.ds(k * piece, piece)

    for d in range(n_y):
        peer = lax.rem(y + d, n_y)
        columns = [
            rows_ref[:, pl.ds(pl.multiple_of(peer * feats + j * LANES, LANES), LANES)].astype(f32)
            for j in range(n_col)
        ]
        whole = jnp.concatenate(columns + [routing], axis=0).astype(bf16)
        if d == 0:
            held[y] = whole
        else:
            stage[d - 1] = whole

    pl.semaphore_wait(barrier, len(greet))

    def y_copy(d):
        return remote(
            stage.at[d - 1],
            held.at[y],
            y_send.at[d - 1],
            y_recv.at[d - 1],
            dp=lax.rem(y + d, n_y),
        )

    def y_arrival(d):
        sender = lax.rem(y + n_y - d, n_y)
        return remote(
            stage.at[d - 1], held.at[sender], y_send.at[d - 1], y_recv.at[d - 1], dp=sender
        )

    def x_copy(replica):
        j = lax.rem(replica + n_x - x, n_x)
        rows = pl.ds(pl.multiple_of((n_x - j) * piece, UNIT), piece)
        return remote(
            held.at[replica],
            zbuf.at[0, 0, rows],
            x_send.at[j - 1],
            x_recv.at[j - 1],
            node=replica * 2 + core,
        )

    def x_arrival(k):
        sender = lax.rem(x + k, n_x)
        return remote(
            held.at[sender],
            zbuf.at[0, 0, piece_rows(k)],
            x_send.at[n_x - 1 - k],
            x_recv.at[n_x - 1 - k],
            node=sender * 2 + core,
        )

    def z_copy(side, slot, to_side, to_slot, k):
        return remote(
            zbuf.at[side, slot, piece_rows(k)],
            zbuf.at[to_side, to_slot, piece_rows(k)],
            z_send.at[side, slot, k],
            z_recv.at[to_side, to_slot, k],
            local=z_up if side == 0 else z_down,
        )

    def z_own(side, k):
        return remote(
            zbuf.at[0, 0, piece_rows(k)],
            zbuf.at[side, 1, piece_rows(k)],
            z_send.at[side, 0, k],
            z_recv.at[side, 1, k],
            local=z_up if side == 0 else z_down,
        )

    def pass_on(replica):
        @pl.when(replica != x)
        def _():
            x_copy(replica).start()

        @pl.when(replica == x)
        def _():
            zbuf[0, 0, :piece, :] = held[replica]
            for side in range(2):
                z_own(side, 0).start()

    for d in (1, n_y - 1, 2):
        y_copy(d).start()
    pass_on(y)
    for d in (1, n_y - 1, 2):
        y_arrival(d).wait_recv()
        pass_on(lax.rem(y + n_y - d, n_y))
    x_arrival(1).wait_recv()
    z_own(0, 1).start()
    x_arrival(3).wait_recv()
    z_own(1, 3).start()
    z_own(0, 3).start()
    x_arrival(2).wait_recv()
    z_own(1, 2).start()
    z_own(0, 2).start()
    z_own(1, 1).start()
    order = ((0, 1, 3, 2), (0, 3, 2, 1))

    def h_copy(d):
        return remote(
            hidden_ref,
            hid_all.at[y],
            h_send.at[d - 1],
            h_recv.at[d - 1],
            dp=lax.rem(y + d, n_y),
        )

    def h_arrival(d):
        sender = lax.rem(y + n_y - d, n_y)
        return remote(
            hidden_ref, hid_all.at[sender], h_send.at[d - 1], h_recv.at[d - 1], dp=sender
        )

    for d in range(1, n_y):
        h_copy(d).start()
    own_hidden = pltpu.make_async_copy(hidden_ref, hid_all.at[y], h_local)
    own_hidden.start()

    def far_copy(b):
        return remote(far.at[b], far_in.at[b], f_send.at[b], f_recv.at[b], node=sibling)

    def direct_copy(b, j):
        chip = lax.rem(x + j, n_x)
        return remote(
            near.at[b, chip],
            bucket.at[b, x],
            d_send.at[b, j - 1],
            d_recv.at[b, j - 1],
            node=chip * 2 + core,
        )

    def direct_arrival(b, j):
        sender = lax.rem(x + n_x - j, n_x)
        return remote(
            near.at[b, sender],
            bucket.at[b, sender],
            d_send.at[b, j - 1],
            d_recv.at[b, j - 1],
            node=sender * 2 + core,
        )

    chip_of = lax.broadcasted_iota(jnp.int32, (n_x, UNIT, LANES), 0)
    row_of = lax.broadcasted_iota(jnp.int32, (n_x, UNIT, LANES), 1)
    lane_of = lax.broadcasted_iota(jnp.int32, (top, LANES), 1) // lane_group

    def read_block(side, slot):
        block = zbuf[side, slot].astype(f32)
        gap = jnp.zeros((lane_group - n_tok, LANES), f32)
        columns = []
        for j in range(n_col):
            rows = []
            for k in range(n_y):
                start = k * piece + j * n_tok
                rows += [block[start : start + n_tok], gap]
            columns.append(jnp.concatenate(rows, axis=0))
        values = jnp.concatenate(columns, axis=1).astype(bf16)
        parts = []
        for shift in range(3):
            part = jnp.zeros((top, LANES), f32)
            for k in range(n_y):
                held = block[k * piece + data_rows : (k + 1) * piece]
                part = jnp.where(lane_of == (k + shift) % n_y, held, part)
            parts.append(
                pltpu.roll(part, LANES - shift * lane_group, 1) if shift else part
            )
        return values, parts[0] * float(CODE) + parts[1], parts[2]

    def weights(side, codes, gates, which):
        code = ((chip_of * 2 + which) * n_z + z) * CODE + row_of - side * slots
        mine = (row_of >= side * slots) & (row_of < (side + 1) * slots)
        target = jnp.where(mine, code, -1).astype(f32)
        weight = jnp.zeros((n_x, UNIT, LANES), f32)
        for k in range(top):
            weight = weight + jnp.where(
                codes[k : k + 1, :][None] == target, gates[k : k + 1, :][None], 0.0
            )
        return weight.reshape(n_x * UNIT, LANES)

    def place(slot, b, sides):
        blocks = [read_block(side, slot) for side in sides]
        values = jnp.concatenate([values for values, _, _ in blocks], axis=0)
        rows = [
            jnp.concatenate([weights(side, *blocks[side][1:], which) for side in sides], axis=1)
            for which in (1 - core, core)
        ]
        placed = jnp.dot(
            jnp.concatenate(rows, axis=0).astype(bf16), values, preferred_element_type=f32
        ).astype(bf16)
        far[b] = placed[: n_x * UNIT].reshape(n_x, UNIT, feats)
        far_copy(b).start()
        near[b] = placed[n_x * UNIT :].reshape(n_x, UNIT, feats)

    def jump_place(side, step, which):
        if side == 2:
            return lax.rem(z + n_z + jnp.where(which == 0, step, -step), n_z)
        return lax.rem(z + n_z + (step if side == 0 else -step), n_z)

    small_chip = lax.broadcasted_iota(jnp.int32, (n_x, SMALL, LANES), 0)
    small_row = lax.broadcasted_iota(jnp.int32, (n_x, SMALL, LANES), 1)

    def jump_weights(side, codes, gates, which):
        parts = []
        for way, step in JUMPS:
            weight = jnp.zeros((n_x, SMALL, LANES), f32)
            if way in (side, 2):
                code = ((small_chip * 2 + which) * n_z + jump_place(way, step, which)) * CODE
                mine = small_row < slots
                if way == 2:
                    mine = mine & (which == side)
                target = jnp.where(mine, code + small_row, -1).astype(f32)
                for k in range(top):
                    weight = weight + jnp.where(
                        codes[k : k + 1, :][None] == target, gates[k : k + 1, :][None], 0.0
                    )
            parts.append(weight.reshape(n_x * SMALL, LANES))
        return jnp.concatenate(parts, axis=0)

    def place_jumps():
        blocks = [read_block(side, raw) for side in range(2)]
        values = jnp.concatenate([values for values, _, _ in blocks], axis=0)
        gap = jnp.zeros((near_jump.shape[2] - n_col * SMALL, LANES), f32)
        for which, dest in ((1 - core, far_jump), (core, near_jump)):
            rows = [jump_weights(side, *blocks[side][1:], which) for side in range(2)]
            placed = jnp.dot(
                jnp.concatenate(rows, axis=1).astype(bf16), values, preferred_element_type=f32
            )
            for g in range(len(JUMPS)):
                for chip in range(n_x):
                    start = (g * n_x + chip) * SMALL
                    part = placed[start : start + SMALL]
                    columns = [part[:, j * LANES : (j + 1) * LANES] for j in range(n_col)]
                    dest[g, chip] = jnp.concatenate(columns + [gap], axis=0).astype(bf16)
                if dest is far_jump:
                    far_jump_copy(g).start()

    def far_jump_copy(g):
        return remote(
            far_jump.at[g], far_jump_in.at[g], g_send.at[g], g_recv.at[g], node=sibling
        )

    def jump_copy(g, j):
        chip = lax.rem(x + j, n_x)
        return remote(
            near_jump.at[g, chip],
            jump_in.at[g, x],
            j_send.at[g, j],
            j_recv.at[g, j],
            node=chip * 2 + core,
            local=jump_place(*JUMPS[g], core),
        )

    def jump_arrival(g, j):
        sender = lax.rem(x + n_x - j, n_x)
        way, step = JUMPS[g]
        return remote(
            near_jump.at[g, sender],
            jump_in.at[g, sender],
            j_send.at[g, j],
            j_recv.at[g, j],
            node=sender * 2 + core,
            local=jump_place(way, -step, core),
        )

    def merge_jumps():
        for g in range(len(JUMPS)):
            far_jump_copy(g).wait_recv()
            near_jump[g] = near_jump[g] + far_jump_in[g]
            for j in (2, 1, 3, 0):
                jump_copy(g, j).start()

    def finish_jumps():
        for g in (3, 4, 1, 2, 0):
            rows = []
            for j in range(n_x):
                jump_arrival(g, j).wait_recv()
            for replica in range(n_y):
                part = jump_in[g, replica].astype(f32)
                rows.append(
                    jnp.concatenate(
                        [part[j * SMALL : (j + 1) * SMALL] for j in range(n_col)], axis=1
                    )
                )
            count = n_y * SMALL
            bucket_jump[g * count : (g + 1) * count, :] = jnp.concatenate(rows, axis=0).astype(bf16)

    def merge(b):
        far_copy(b).wait_recv()
        near[b] = near[b] + far_in[b]
        for j in (2, 1, 3):
            direct_copy(b, j).start()
        bucket[b, x] = near[b, x]

    def finish(b):
        for j in range(1, n_x):
            direct_arrival(b, j).wait_recv()

    positions = n_y * n_z * slots
    group = GROUP * n_y * UNIT

    def choose(column, start):
        count = column.shape[0]
        pick = lax.broadcasted_iota(jnp.int32, (count, positions), 1) == column
        hid_perm[pl.ds(start, count), :] = jnp.dot(
            pick.astype(bf16),
            hid_all[...].reshape(positions, hid_all.shape[2]),
            preferred_element_type=f32,
        ).astype(bf16)

    def unit_columns(count, first):
        i = lax.broadcasted_iota(jnp.int32, (count, 1), 0)
        unit = lax.div(i, n_y * UNIT) + first
        replica = lax.rem(lax.div(i, UNIT), n_y)
        at = lax.rem(i, UNIT)
        above = at >= slots
        step = jnp.where(unit < raw, unit + 1, 0)
        source = lax.rem(jnp.where(above, z + step, z - step + n_z), n_z)
        column = replica * (n_z * slots) + source * slots + jnp.where(above, at - slots, at)
        used = jnp.where(unit < raw, 2 * slots, slots)
        return jnp.where(at < used, column, -1)

    def order_hidden(g):
        choose(unit_columns(group, g * GROUP), pl.multiple_of(g * group, UNIT))

    def order_hidden_rest():
        full = raw // GROUP * GROUP
        choose(unit_columns((n_unit - full) * n_y * UNIT, full), full * n_y * UNIT)
        parts = []
        for way, step in JUMPS:
            i = lax.broadcasted_iota(jnp.int32, (n_y * SMALL, 1), 0)
            replica, at = lax.div(i, SMALL), lax.rem(i, SMALL)
            far_off = raw + step
            source = lax.rem(z + far_off if way == 1 else z + n_z - far_off, n_z)
            column = replica * (n_z * slots) + source * slots + at
            parts.append(jnp.where(at < slots, column, -1))
        choose(jnp.concatenate(parts, axis=0), n_unit * n_y * UNIT)

    def product(low, high, j):
        cols = pl.ds(pl.multiple_of(j * LANES, LANES), LANES)
        start, stop = low * n_y * UNIT, high * n_y * UNIT
        if low == n_unit:
            stop = hid_perm.shape[0]
            left = bucket_jump[:, cols]
        else:
            left = bucket[low:high, :, :, cols].reshape(stop - start, LANES)
        term = lax.dot_general(
            left,
            hid_perm[start:stop, :],
            (((0,), (0,)), ((), ())),
            preferred_element_type=f32,
        )
        if low > 0:
            term = term + acc[cols, :]
        if low < n_unit:
            acc[cols, :] = term
        else:
            out_ref[cols, :] = term.astype(bf16)

    def products(low, high):
        @pl.loop(0, n_col)
        def _(j):
            product(low, high, j)

    hidden_at = 6
    first_at = hidden_at + 2
    second_at = first_at + (n_col + 1) // 2
    place(0, raw, (0,))

    @pl.loop(1, raw + 1)
    def _(t):
        def z_step(at):
            for side in range(2):
                k = order[side][at]
                z_copy(side, t - 1, side, t, k).wait_recv()

                @pl.when(t < raw)
                def _():
                    z_copy(side, t, side, t + 1, k).start()

        z_step(0)
        z_step(1)

        @pl.when(t > 1)
        def _():
            merge(t - 2)

        @pl.when(t == 1)
        def _():
            merge(raw)

        z_step(2)

        @pl.when(t == hidden_at)
        def _():
            for d in range(1, n_y):
                h_arrival(d).wait_recv()
            own_hidden.wait()

        @pl.when((t > hidden_at) & (t <= hidden_at + raw // GROUP))
        def _():
            order_hidden(t - hidden_at - 1)

        @pl.when(t == hidden_at + raw // GROUP + 1)
        def _():
            order_hidden_rest()

        @pl.when((t >= first_at) & (t < second_at))
        def _():
            j = (t - first_at) * 2
            product(0, GROUP, j)

            @pl.when(j + 1 < n_col)
            def _():
                product(0, GROUP, j + 1)

        @pl.when(t >= second_at)
        def _():
            j = (t - second_at) * 2
            product(GROUP, 2 * GROUP, j)
            product(GROUP, 2 * GROUP, j + 1)

        z_step(3)

        @pl.when(t == raw)
        def _():
            place_jumps()

        place(t, t - 1, (0, 1))

        @pl.when(t > 2)
        def _():
            finish(t - 3)

    merge_jumps()
    merge(raw - 1)
    finish(raw)
    for j in range(2 * (raw + 1 - second_at), n_col):
        product(GROUP, 2 * GROUP, j)
    finish(raw - 2)
    products(2 * GROUP, 3 * GROUP)
    finish(raw - 1)
    products(3 * GROUP, n_unit)
    finish_jumps()
    products(n_unit, n_unit + 1)

    for d in range(1, n_y):
        y_copy(d).wait_send()
        h_copy(d).wait_send()
    for k in range(n_y):
        for side in range(2):
            z_own(side, k).wait_send()

            @pl.loop(1, raw)
            def _(t):
                z_copy(side, t, side, t + 1, k).wait_send()

    for j in range(1, n_x):
        x_copy(lax.rem(x + j, n_x)).wait_send()

    @pl.loop(0, n_unit)
    def _(b):
        far_copy(b).wait_send()
        for j in range(1, n_x):
            direct_copy(b, j).wait_send()

    for g in range(len(JUMPS)):
        far_jump_copy(g).wait_send()
        for j in range(n_x):
            jump_copy(g, j).wait_send()


def shards(grad_out, expert_ids, slot_ids, gate_values, hidden):
    n_x = lax.axis_size("node") // 2
    n_z, n_y = lax.axis_size("local"), lax.axis_size("dp")
    n_tok, width = grad_out.shape
    top = expert_ids.shape[1]
    _, capacity, units = hidden.shape
    feats = width // n_y
    raw = n_z // 2 - AHEAD
    n_unit = raw + 1
    jump_rows = pl.cdiv(feats // LANES * SMALL, UNIT) * UNIT
    piece = feats // LANES * n_tok + top
    bf16 = jnp.bfloat16
    vmem = pl.BlockSpec(memory_space=pltpu.VMEM)
    dma = pltpu.SemaphoreType.DMA
    result = pl.pallas_call(
        kernel,
        out_shape=pltpu.VMEM((feats, units), bf16),
        in_specs=[vmem] * 4 + [pl.BlockSpec(memory_space=pl.ANY)],
        out_specs=vmem,
        scratch_shapes=[
            pltpu.VMEM((n_y - 1, piece, LANES), bf16),
            pltpu.VMEM((n_y, piece, LANES), bf16),
            pltpu.VMEM((2, raw + 1, n_y * piece, LANES), bf16),
            pltpu.VMEM((n_unit, n_x, UNIT, feats), bf16),
            pltpu.VMEM((n_unit, n_x, UNIT, feats), bf16),
            pltpu.VMEM((n_unit, n_x, UNIT, feats), bf16),
            pltpu.VMEM((len(JUMPS), n_x, jump_rows, LANES), bf16),
            pltpu.VMEM((len(JUMPS), n_x, jump_rows, LANES), bf16),
            pltpu.VMEM((len(JUMPS), n_x, jump_rows, LANES), bf16),
            pltpu.VMEM((len(JUMPS), n_x, jump_rows, LANES), bf16),
            pltpu.VMEM((n_unit, n_y, UNIT, feats), bf16),
            pltpu.VMEM((len(JUMPS) * n_y * SMALL, feats), bf16),
            pltpu.VMEM((n_y, capacity, units), bf16),
            pltpu.VMEM((n_unit * n_y * UNIT + len(JUMPS) * n_y * SMALL, units), bf16),
            pltpu.VMEM((feats, units), jnp.float32),
            dma((n_y - 1,)),
            dma((n_y - 1,)),
            dma((n_x - 1,)),
            dma((n_x - 1,)),
            dma((n_y - 1,)),
            dma((n_y - 1,)),
            dma,
            dma((2, raw + 1, n_y)),
            dma((2, raw + 1, n_y)),
            dma((n_unit,)),
            dma((n_unit,)),
            dma((n_unit, n_x - 1)),
            dma((n_unit, n_x - 1)),
            dma((len(JUMPS),)),
            dma((len(JUMPS),)),
            dma((len(JUMPS), n_x)),
            dma((len(JUMPS), n_x)),
        ],
        compiler_params=pltpu.CompilerParams(
            collective_id=0, has_side_effects=True, vmem_limit_bytes=56 * 1024 * 1024
        ),
        cost_estimate=pl.CostEstimate(
            flops=2 * n_y * capacity * feats * units, bytes_accessed=4 << 20, transcendentals=0
        ),
    )(grad_out, expert_ids.T, slot_ids.T, gate_values.T, hidden[0])
    return result[None]


def solution(mesh):
    in_specs = (
        P(("node", "local", "dp"), None),
        P(("node", "local", "dp"), None),
        P(("node", "local", "dp"), None),
        P(("node", "local", "dp"), None),
        P(("node", "local"), "dp", None),
    )
    out_specs = P(("node", "local"), "dp", None)
    return jax.shard_map(shards, mesh=mesh, in_specs=in_specs, out_specs=out_specs, check_vma=False)
```

time: 109 us -> 102 us (0.936)
  Pallas kernels: 106 us -> 100 us
  local copies, waits for them, and re-layouts: 2.87 us -> 1.23 us
    pallas_call x1, Pallas kernels: 106 us -> 100 us  [shards(): pl.pallas_call(kernel, out_shape=pltpu.VMEM((feats, units), bf16), in_spe...]
    unnamed x1, local copies, waits for them, and re-layouts: 2.87 us -> 1.23 us
where the time goes in v3:
time: 102 us; the launch traced here: 101 us
  Pallas kernels  100 us (98%)
  local copies, waits for them, and re-layouts  1.23 us (1%)
    pallas_call x1, Pallas kernels, shards(): pl.pallas_call(kernel, out_shape=pltpu.VMEM((feats, units), bf16), in_spe...  100 us

profile of v3, /device:TPU:1, one launch (start us, length us, event | category | flops | bytes accessed | tf_op | source)
XLA Modules:
  0.0 101.2 jit_solution(12283962219782420147)
XLA Ops:
  0.0 100.0 %shard_map.55 = bf16[896,1024]{1,0:T(8,128)(2,1)S(1)} custom-call(bf16[24,3584]{1,0:T(8,128)(2,1)} %rows_ref.1, s32[8,24]{1,0:T(8,128)} %bitcast.7, s32[8,24]{1,0:T(8,128)} %bitcast.8, bf16[8,24]{1,0:T(8,128)(2,1)} %bitcast.9, bf16[192,1024]{1,0:T(8,128)(2,1)} %bitcast.6), custom_call_target="tpu_custom_call" | custom-call | flops 1409286144 | bytes 4194304 | tf_op jit(solution)/shard_map/pallas_call | solution.py:601
  100.0 1.2 %copy.7 = bf16[1,896,1024]{2,1,0:T(8,128)(2,1)} copy(bf16[1,896,1024]{2,1,0:T(8,128)(2,1)S(1)} %bitcast.5) | data formatting | bytes 3670016
